TPU v7x, 256 devices: a whole 4x4x8 slice. The times are simulated.
256 devices in a mesh: dp: 4 (over x), vocab: 64 (over y, z, core).
Axes of the slice: x: 4, y: 4, z: 8, core: 2. Of those that a mesh axis runs over, the one named last changes fastest.
Arguments:
- features: bfloat16 [2048, 4096], P(('dp', 'vocab')), may hold values from -8 to 8
- head: bfloat16 [65536, 4096], P(('dp', 'vocab')), may hold values from -0.5 to 0.5
- momentum: bfloat16 [65536, 4096], P(('dp', 'vocab')), may hold values from -7.124618e-08 to 7.124618e-08
- hessian: bfloat16 [65536, 4096], P(('dp', 'vocab')), may hold values from 4.765752e-10 to 4.7683716e-06
- true_labels: int32 [2048], replicated, may hold values from 0 to 65535
- sampled_labels: int32 [2048], replicated, may hold values from 0 to 65535
Outputs:
- mean_loss: float32 [], replicated
- new_hessian: bfloat16 [65536, 4096], P(('dp', 'vocab'))
- update: bfloat16 [65536, 4096], P(('dp', 'vocab'))
All inputs are finite; a program needn't handle non-finite values.
Results may differ from a plain program's by a relative error of at most 0.019.
Values may be sent and summed in bfloat16 or wider, within the bound.
A program may use at most 128 MiB of HBM per device.

v0:
```python
import jax
import jax.numpy as jnp
from jax import lax
from jax.sharding import PartitionSpec as P

hess_decay = 0.99
clip_scale = 0.05


def local_stats(logits, columns, labels):
    highest = jnp.max(logits, axis=1)
    row_total = jnp.sum(jnp.exp(logits - highest[:, None]), axis=1)
    picked = jnp.sum(jnp.where(columns[None, :] == labels[:, None], logits, 0.0), axis=1)
    return (highest, row_total, picked)


def make_signal(logits, log_norm, columns, labels):
    chosen = (columns[None, :] == labels[:, None]).astype(jnp.float32)
    return (jnp.exp(logits - log_norm[:, None]) - chosen).astype(jnp.bfloat16)


def sophia_tail(gradient, momentum, hessian):
    fresh = hess_decay * hessian.astype(jnp.float32) + (1.0 - hess_decay) * gradient * gradient
    clipped = jnp.clip(momentum.astype(jnp.float32) / (clip_scale * fresh), -1.0, 1.0)
    return (fresh.astype(jnp.bfloat16), clipped.astype(jnp.bfloat16))


def shards(features, head, momentum, hessian, true_labels, sampled_labels):
    voc_dev = head.shape[0]
    every_row = lax.all_gather(features, ("dp", "vocab"), axis=0, tiled=True)
    logits = lax.dot_general(
        every_row, head, (((1,), (1,)), ((), ())), preferred_element_type=jnp.float32
    )
    own_offset = (lax.axis_index("dp") * lax.axis_size("vocab") + lax.axis_index("vocab")) * voc_dev
    columns = own_offset + jnp.arange(voc_dev, dtype=jnp.int32)
    highest, row_total, picked = local_stats(logits, columns, true_labels)
    top_all = lax.pmax(highest, ("dp", "vocab"))
    row_total, picked = lax.psum((row_total * jnp.exp(highest - top_all), picked), ("dp", "vocab"))
    highest = top_all
    log_norm = highest + jnp.log(row_total)
    mean_loss = jnp.mean(log_norm - picked)
    signal = make_signal(logits, log_norm, columns, sampled_labels)
    groups = lax.axis_size("dp")
    signal_groups = signal.reshape(groups, -1, voc_dev)
    row_groups = every_row.reshape(groups, -1, every_row.shape[1])
    partials = lax.dot_general(
        signal_groups, row_groups, (((1,), (1,)), ((0,), (0,))), preferred_element_type=jnp.float32
    )
    rounded = lax.optimization_barrier(partials.astype(jnp.bfloat16)).astype(jnp.float32)
    gradient = jnp.sum(rounded, axis=0)
    fresh, clipped = sophia_tail(gradient, momentum, hessian)
    return (mean_loss, fresh, clipped)


def solution(mesh):
    in_specs = (
        P(("dp", "vocab"), None),
        P(("dp", "vocab"), None),
        P(("dp", "vocab"), None),
        P(("dp", "vocab"), None),
        P(),
        P(),
    )
    out_specs = (P(), P(("dp", "vocab"), None), P(("dp", "vocab"), None))
    return jax.shard_map(shards, mesh=mesh, in_specs=in_specs, out_specs=out_specs, check_vma=False)
```

profile of v0, /device:TPU:1, one launch (start us, length us, event | category | flops | bytes accessed | tf_op | source)
XLA Modules:
  0.0 339.7 jit_solution(14028145733843676023)
XLA Ops:
  7.2 0.0 copy-start
  7.2 0.0 all-gather.2.cloned.1.call-start
  7.2 0.7 all-gather.2.cloned.1.call-update
  7.9 0.0 copy-start.1
  7.9 133.0 %all-gather.2.cloned.1.call-done = bf16[2048,4096]{1,0:T(8,128)(2,1)} async-done(((bf16[8,4096]{1,0:T(8,128)(2,1)}), bf16[2048,4096]{1,0:T(8,128)(2,1)}) %all-gather.2.cloned.1.call-update) | async-done | bytes 16777232 | tf_op jit(solution)/shard_map/all_gather | solution.py:30
  140.9 0.0 copy-done
  140.9 9.8 %fusion.2 = (f32[2048]{0:T(1024)S(1)}, f32[2048,256]{1,0:T(8,128)}) fusion(bf16[2048,4096]{1,0:T(8,128)(2,1)} %all-gather.2.cloned.1.call-done, bf16[256,4096]{1,0:T(8,128)(2,1)S(1)} %copy-done), kind=kOutput, calls=%fused_computation.13 | convolution fusion | flops 4295489536 | bytes 20979712 | tf_op jit(solution)/shard_map/dot_general | solution.py:31
  150.8 0.0 copy-start.2
  150.8 74.4 %pmax.7 = f32[2048]{0:T(1024)S(1)} all-reduce(f32[2048]{0:T(1024)S(1)} %get-tuple-element.11), channel_id=1, replica_groups=mesh['dp'=4,'vocab'=64] {'dp','vocab'}, use_global_device_ids=true, to_apply=%region_1.0 | all-reduce | flops 2048 | bytes 16384 | tf_op jit(solution)/shard_map/pmax | solution.py:37
  225.2 0.0 copy-done.1
  225.2 2.5 select_reduce_fusion
  227.7 73.8 %all-reduce = (f32[2048]{0:T(1024)S(1)}, f32[2048]{0:T(1024)S(1)}) all-reduce(f32[2048]{0:T(1024)S(1)} %exponential_multiply_fusion, f32[2048]{0:T(1024)S(1)} %get-tuple-element.3), channel_id=1, replica_groups=mesh['dp'=4,'vocab'=64] {'dp','vocab'}, use_global_device_ids=true, to_apply=%region_3.4 | all-reduce | flops 4096 | bytes 32768 | tf_op jit(solution)/shard_map/psum | solution.py:38
  301.5 0.6 subtract_reduce_fusion
  302.1 0.0 copy-done.2
  302.2 1.9 subtract_convert_fusion
  304.1 12.6 %convolution_convert_fusion = bf16[4,256,4096]{2,1,0:T(8,128)(2,1)} fusion(bf16[4,512,256]{2,1,0:T(8,128)(2,1)S(1)} %bitcast.7, bf16[4,512,4096]{2,1,0:T(8,128)(2,1)} %bitcast.6), kind=kOutput, calls=%fused_computation.1 | convolution fusion | flops 4299161600 | bytes 26214400 | tf_op jit(solution)/shard_map/dot_general | solution.py:46
  316.7 7.3 %convert_reduce_fusion = f32[256,4096]{1,0:T(8,128)} fusion(bf16[4,256,4096]{2,1,0:T(8,128)(2,1)} %convolution_convert_fusion), kind=kLoop, calls=%fused_computation | loop fusion | flops 7340032 | bytes 12582912 | tf_op jit(solution)/shard_map/reduce_sum | solution.py:50
  324.6 7.1 %clamp_convert_fusion = (bf16[256,4096]{1,0:T(8,128)(2,1)}, bf16[256,4096]{1,0:T(8,128)(2,1)}) fusion(bf16[256,4096]{1,0:T(8,128)(2,1)} %param.8, f32[256,4096]{1,0:T(8,128)} %convert_reduce_fusion, bf16[256,4096]{1,0:T(8,128)(2,1)} %param.9), kind=kLoop, calls=%fused_computation.4 | loop fusion | flops 11534336 | bytes 12582912 | tf_op jit(solution)/shard_map/convert_element_type | solution.py:25
  (2 shorter events, 0.0 us)
Async XLA Ops:
  7.2 133.7 %copy-start = (bf16[256,4096]{1,0:T(8,128)(2,1)S(1)}, bf16[256,4096]{1,0:T(8,128)(2,1)}, u32[]{:S(2)}) copy-start(bf16[256,4096]{1,0:T(8,128)(2,1)} %param.7) | copy-start | bytes 6291460
  7.2 133.7 %all-gather.2.cloned.1.call-start = ((), (), s32[]{:S(2)}) async-start(), calls=%async_computation | async-start | bytes 16842752 | tf_op jit(solution)/shard_map/all_gather | solution.py:30
  7.9 217.3 %copy-start.1 = (s32[2048]{0:T(1024)S(1)}, s32[2048]{0:T(1024)}, u32[]{:S(2)}) copy-start(s32[2048]{0:T(1024)} %param.10) | copy-start | bytes 24580
  150.8 151.4 %copy-start.2 = (s32[2048]{0:T(1024)S(1)}, s32[2048]{0:T(1024)}, u32[]{:S(2)}) copy-start(s32[2048]{0:T(1024)} %param.11) | copy-start | bytes 24580
Sparse Core Ops, SparseCore 0:
  11.7 129.1 all-gather.1
where the time goes:
time: 340 us
  blocking collectives  148 us (44%)
  waiting for transfers between devices  134 us (39%)
  matrix products  22.5 us (7%)
  other arithmetic  19.5 us (6%)
  between operations  15.9 us (5%)
    all_gather x1, waiting for transfers between devices, shards(): every_row = lax.all_gather(features, ('dp', 'vocab'), axis=0, tiled=True)  133 us
    pmax x1, blocking collectives, shards(): top_all = lax.pmax(highest, ('dp', 'vocab'))  74.4 us
    psum x1, blocking collectives, shards(): lax.psum((row_total * jnp.exp(highest - top_all), picked), ('dp', 'vocab'))  73.8 us
    dot_general x1, matrix products, shards(): lax.dot_general(signal_groups, row_groups, (((1,), (1,)), ((0,), (0,))),...  12.6 us
    dot_general x1, matrix products, shards(): lax.dot_general(every_row, head, (((1,), (1,)), ((), ())), preferred_elem...  9.85 us
    reduce_sum x1, other arithmetic, shards(): gradient = jnp.sum(rounded, axis=0)  7.29 us
    convert_element_type x1, other arithmetic, sophia_tail(): return (fresh.astype(jnp.bfloat16), clipped.astype(jnp.bfloat16))  7.12 us
  transfers between devices with their start and end apart: 1, of which 1 were waited for; matrix products, arithmetic and copies ran while one was open for 0% of the time, Pallas kernels for 0%

commit v1 on v0

--- a/solution.py
+++ b/solution.py
@@ -35,7 +35,9 @@
     columns = own_offset + jnp.arange(voc_dev, dtype=jnp.int32)
     highest, row_total, picked = local_stats(logits, columns, true_labels)
     top_all = lax.pmax(highest, ("dp", "vocab"))
-    row_total, picked = lax.psum((row_total * jnp.exp(highest - top_all), picked), ("dp", "vocab"))
+    row_total, picked = lax.psum(
+        lax.psum((row_total * jnp.exp(highest - top_all), picked), "vocab"), "dp"
+    )
     highest = top_all
     log_norm = highest + jnp.log(row_total)
     mean_loss = jnp.mean(log_norm - picked)

time: 340 us -> 528 us (1.55); the launches traced: 340 us -> 521 us
  blocking collectives: 148 us -> 329 us
    psum x1 -> x2, blocking collectives: 73.8 us -> 255 us  [the longest x1 244 us: shards(): lax.psum((row_total * jnp.exp(highest - top_all), picked), 'vocab')]
where the time goes in v1:
time: 528 us; the launch traced here: 521 us
  blocking collectives  329 us (62%)
  waiting for transfers between devices  134 us (25%)
  matrix products  22.5 us (4%)
  other arithmetic  19.5 us (4%)
  between operations  15.9 us (3%)
    psum x1, blocking collectives, shards(): lax.psum((row_total * jnp.exp(highest - top_all), picked), 'vocab')  244 us
    all_gather x1, waiting for transfers between devices, shards(): every_row = lax.all_gather(features, ('dp', 'vocab'), axis=0, tiled=True)  133 us
    pmax x1, blocking collectives, shards(): top_all = lax.pmax(highest, ('dp', 'vocab'))  74.4 us
    dot_general x1, matrix products, shards(): lax.dot_general(signal_groups, row_groups, (((1,), (1,)), ((0,), (0,))),...  12.6 us
    psum x1, blocking collectives, shards(): lax.psum(lax.psum((row_total * jnp.exp(highest - top_all), picked), 'voca...  10.8 us
  transfers between devices with their start and end apart: 1, of which 1 were waited for; matrix products, arithmetic and copies ran while one was open for 0% of the time, Pallas kernels for 0%

profile of v1, /device:TPU:1, one launch (start us, length us, event | category | flops | bytes accessed | tf_op | source)
XLA Modules:
  0.0 520.5 jit_solution(6046948159408463144)
XLA Ops:
  7.2 0.0 copy-start
  7.2 0.0 all-gather.2.cloned.1.call-start
  7.2 0.7 all-gather.2.cloned.1.call-update
  7.9 0.0 copy-start.1
  7.9 133.0 %all-gather.2.cloned.1.call-done = bf16[2048,4096]{1,0:T(8,128)(2,1)} async-done(((bf16[8,4096]{1,0:T(8,128)(2,1)}), bf16[2048,4096]{1,0:T(8,128)(2,1)}) %all-gather.2.cloned.1.call-update) | async-done | bytes 16777232 | tf_op jit(solution)/shard_map/all_gather | solution.py:30
  140.9 0.0 copy-done
  140.9 9.8 %fusion.2 = (f32[2048]{0:T(1024)S(1)}, f32[2048,256]{1,0:T(8,128)}) fusion(bf16[2048,4096]{1,0:T(8,128)(2,1)} %all-gather.2.cloned.1.call-done, bf16[256,4096]{1,0:T(8,128)(2,1)S(1)} %copy-done), kind=kOutput, calls=%fused_computation.13 | convolution fusion | flops 4295489536 | bytes 20979712 | tf_op jit(solution)/shard_map/dot_general | solution.py:31
  150.8 0.0 copy-start.2
  150.8 74.4 %pmax.7 = f32[2048]{0:T(1024)S(1)} all-reduce(f32[2048]{0:T(1024)S(1)} %get-tuple-element.13), channel_id=1, replica_groups=mesh['dp'=4,'vocab'=64] {'dp','vocab'}, use_global_device_ids=true, to_apply=%region_1.0 | all-reduce | flops 2048 | bytes 16384 | tf_op jit(solution)/shard_map/pmax | solution.py:37
  225.2 0.0 copy-done.1
  225.2 2.5 select_reduce_fusion
  227.7 243.8 %all-reduce = (f32[2048]{0:T(1024)S(1)}, f32[2048]{0:T(1024)S(1)}) all-reduce(f32[2048]{0:T(1024)S(1)} %exponential_multiply_fusion, f32[2048]{0:T(1024)S(1)} %get-tuple-element.3), channel_id=1, replica_groups=mesh['dp'=4,'vocab'=64] {'vocab'}, use_global_device_ids=true, to_apply=%region_3.4 | all-reduce | flops 4096 | bytes 32768 | tf_op jit(solution)/shard_map/psum | solution.py:39
  471.5 10.8 %all-reduce.1 = (f32[2048]{0:T(1024)S(1)}, f32[2048]{0:T(1024)S(1)}) all-reduce(f32[2048]{0:T(1024)S(1)} %get-tuple-element.5, f32[2048]{0:T(1024)S(1)} %get-tuple-element.6), channel_id=1, replica_groups=mesh['dp'=4,'vocab'=64] {'dp'}, use_global_device_ids=true, to_apply=%region_4.5 | all-reduce | flops 4096 | bytes 32768 | tf_op jit(solution)/shard_map/psum | solution.py:38
  482.3 0.6 subtract_reduce_fusion
  482.9 0.0 copy-done.2
  482.9 1.9 subtract_convert_fusion
  484.9 12.6 %convolution_convert_fusion = bf16[4,256,4096]{2,1,0:T(8,128)(2,1)} fusion(bf16[4,512,256]{2,1,0:T(8,128)(2,1)S(1)} %bitcast.7, bf16[4,512,4096]{2,1,0:T(8,128)(2,1)} %bitcast.6), kind=kOutput, calls=%fused_computation.1 | convolution fusion | flops 4299161600 | bytes 26214400 | tf_op jit(solution)/shard_map/dot_general | solution.py:48
  497.5 7.3 %convert_reduce_fusion = f32[256,4096]{1,0:T(8,128)} fusion(bf16[4,256,4096]{2,1,0:T(8,128)(2,1)} %convolution_convert_fusion), kind=kLoop, calls=%fused_computation | loop fusion | flops 7340032 | bytes 12582912 | tf_op jit(solution)/shard_map/reduce_sum | solution.py:52
  505.4 7.1 %clamp_convert_fusion = (bf16[256,4096]{1,0:T(8,128)(2,1)}, bf16[256,4096]{1,0:T(8,128)(2,1)}) fusion(bf16[256,4096]{1,0:T(8,128)(2,1)} %param.8, f32[256,4096]{1,0:T(8,128)} %convert_reduce_fusion, bf16[256,4096]{1,0:T(8,128)(2,1)} %param.9), kind=kLoop, calls=%fused_computation.4 | loop fusion | flops 11534336 | bytes 12582912 | tf_op jit(solution)/shard_map/convert_element_type | solution.py:25
  (2 shorter events, 0.0 us)
Async XLA Ops:
  7.2 133.7 %copy-start = (bf16[256,4096]{1,0:T(8,128)(2,1)S(1)}, bf16[256,4096]{1,0:T(8,128)(2,1)}, u32[]{:S(2)}) copy-start(bf16[256,4096]{1,0:T(8,128)(2,1)} %param.7) | copy-start | bytes 6291460
  7.2 133.7 %all-gather.2.cloned.1.call-start = ((), (), s32[]{:S(2)}) async-start(), calls=%async_computation | async-start | bytes 16842752 | tf_op jit(solution)/shard_map/all_gather | solution.py:30
  7.9 217.2 %copy-start.1 = (s32[2048]{0:T(1024)S(1)}, s32[2048]{0:T(1024)}, u32[]{:S(2)}) copy-start(s32[2048]{0:T(1024)} %param.10) | copy-start | bytes 24580
  150.8 332.2 %copy-start.2 = (s32[2048]{0:T(1024)S(1)}, s32[2048]{0:T(1024)}, u32[]{:S(2)}) copy-start(s32[2048]{0:T(1024)} %param.11) | copy-start | bytes 24580
Sparse Core Ops, SparseCore 0:
  11.7 129.1 all-gather.1

commit v2 on v0

--- a/solution.py
+++ b/solution.py
@@ -27,7 +27,12 @@
 
 def shards(features, head, momentum, hessian, true_labels, sampled_labels):
     voc_dev = head.shape[0]
-    every_row = lax.all_gather(features, ("dp", "vocab"), axis=0, tiled=True)
+    every_row = jnp.concatenate(
+        lax.all_to_all(
+            jnp.stack([features] * lax.axis_size(("dp", "vocab"))), ("dp", "vocab"), 0, 0
+        ),
+        axis=0,
+    )
     logits = lax.dot_general(
         every_row, head, (((1,), (1,)), ((), ())), preferred_element_type=jnp.float32
     )

time: 340 us -> 583 us (1.71)
  waiting for transfers between devices: 134 us -> 368 us
  starting transfers between devices: 0.04 us -> 16.7 us
  between operations: 15.9 us -> 2.49 us
  local copies, waits for them, and re-layouts: 0.02 us -> 6.81 us
    all_to_all x0 -> x1, waiting for transfers between devices: none -> 368 us  [shards(): lax.all_to_all(jnp.stack([features] * lax.axis_size(('dp', 'vocab'))), ('...]
    all_gather x1 -> x0, waiting for transfers between devices: 133 us -> none  [shards(): every_row = lax.all_gather(features, ('dp', 'vocab'), axis=0, tiled=True)]
    all_to_all x0 -> x1, starting transfers between devices: none -> 16.7 us  [shards(): lax.all_to_all(jnp.stack([features] * lax.axis_size(('dp', 'vocab'))), ('...]
    another operation x0 -> x1, local copies, waits for them, and re-layouts: none -> 6.79 us  [shards(): jnp.stack([features] * lax.axis_size(('dp', 'vocab')))]
where the time goes in v2:
time: 583 us
  waiting for transfers between devices  368 us (63%)
  blocking collectives  147 us (25%)
  matrix products  22.5 us (4%)
  other arithmetic  19.5 us (3%)
  starting transfers between devices  16.7 us (3%)
  local copies, waits for them, and re-layouts  6.81 us (1%)
    all_to_all x1, waiting for transfers between devices, shards(): lax.all_to_all(jnp.stack([features] * lax.axis_size(('dp', 'vocab'))), ('...  368 us
    psum x1, blocking collectives, shards(): lax.psum((row_total * jnp.exp(highest - top_all), picked), ('dp', 'vocab'))  74.6 us
    pmax x1, blocking collectives, shards(): top_all = lax.pmax(highest, ('dp', 'vocab'))  72.2 us
    all_to_all x1, starting transfers between devices, shards(): lax.all_to_all(jnp.stack([features] * lax.axis_size(('dp', 'vocab'))), ('...  16.7 us
    dot_general x1, matrix products, shards(): lax.dot_general(signal_groups, row_groups, (((1,), (1,)), ((0,), (0,))),...  12.6 us
  transfers between devices with their start and end apart: 1, of which 1 were waited for; matrix products, arithmetic and copies ran while one was open for 0% of the time, Pallas kernels for 0%

profile of v2, /device:TPU:1, one launch (start us, length us, event | category | flops | bytes accessed | tf_op | source)
XLA Modules:
  0.0 582.6 jit_solution(14914979208728636641)
XLA Ops:
  0.6 0.0 copy-start
  0.6 6.8 %stack.2 = bf16[256,8,4096]{2,1,0:T(8,128)(2,1)} broadcast(bf16[8,4096]{1,0:T(8,128)(2,1)} %param.6), dimensions={1,2} | broadcast | bytes 16842752 | tf_op jit(solution)/shard_map/stack | solution.py:32
  7.4 16.7 %all-to-all-start = ((bf16[256,8,4096]{2,1,0:T(8,128)(2,1)}), bf16[256,8,4096]{2,1,0:T(8,128)(2,1)}, u32[]{:S(2)}, u32[]{:S(2)}) async-start(bf16[256,8,4096]{2,1,0:T(8,128)(2,1)} %stack.2), calls=%async_computation | async-start | bytes 33554432 | tf_op jit(solution)/shard_map/all_to_all | solution.py:31
  24.1 0.0 copy-start.1
  24.1 0.0 copy-start.2
  24.1 367.9 %all-to-all-done = bf16[256,8,4096]{2,1,0:T(8,128)(2,1)} async-done(((bf16[256,8,4096]{2,1,0:T(8,128)(2,1)}), bf16[256,8,4096]{2,1,0:T(8,128)(2,1)}, u32[]{:S(2)}, u32[]{:S(2)}) %all-to-all-start) | async-done | bytes 16777248 | tf_op jit(solution)/shard_map/all_to_all | solution.py:31
  392.0 0.0 copy-done
  392.0 9.8 %fusion.4 = (f32[2048]{0:T(1024)S(1)}, f32[2048,256]{1,0:T(8,128)}) fusion(bf16[256,4096]{1,0:T(8,128)(2,1)S(1)} %copy-done, bf16[256,8,4096]{2,1,0:T(8,128)(2,1)} %all-to-all-done), kind=kOutput, calls=%fused_computation.15 | convolution fusion | flops 4295489536 | bytes 20979712 | tf_op jit(solution)/shard_map/dot_general | solution.py:36
  401.9 72.2 %pmax.7 = f32[2048]{0:T(1024)S(1)} all-reduce(f32[2048]{0:T(1024)S(1)} %get-tuple-element.11), channel_id=1, replica_groups=mesh['dp'=4,'vocab'=64] {'dp','vocab'}, use_global_device_ids=true, to_apply=%region_1.0 | all-reduce | flops 2048 | bytes 16384 | tf_op jit(solution)/shard_map/pmax | solution.py:42
  474.1 0.0 copy-done.1
  474.1 2.5 select_reduce_fusion
  476.6 74.6 %all-reduce = (f32[2048]{0:T(1024)S(1)}, f32[2048]{0:T(1024)S(1)}) all-reduce(f32[2048]{0:T(1024)S(1)} %exponential_multiply_fusion, f32[2048]{0:T(1024)S(1)} %get-tuple-element.3), channel_id=1, replica_groups=mesh['dp'=4,'vocab'=64] {'dp','vocab'}, use_global_device_ids=true, to_apply=%region_3.4 | all-reduce | flops 4096 | bytes 32768 | tf_op jit(solution)/shard_map/psum | solution.py:43
  551.2 0.6 subtract_reduce_fusion
  551.8 0.0 copy-done.2
  551.8 1.9 subtract_convert_fusion
  553.7 12.6 %convolution_convert_fusion = bf16[4,256,4096]{2,1,0:T(8,128)(2,1)} fusion(bf16[4,512,256]{2,1,0:T(8,128)(2,1)S(1)} %bitcast.10, bf16[4,512,4096]{2,1,0:T(8,128)(2,1)} %bitcast.2), kind=kOutput, calls=%fused_computation.3 | convolution fusion | flops 4299161600 | bytes 26214400 | tf_op jit(solution)/shard_map/dot_general | solution.py:51
  566.4 7.3 %convert_reduce_fusion = f32[256,4096]{1,0:T(8,128)} fusion(bf16[4,256,4096]{2,1,0:T(8,128)(2,1)} %convolution_convert_fusion), kind=kLoop, calls=%fused_computation.2 | loop fusion | flops 7340032 | bytes 12582912 | tf_op jit(solution)/shard_map/reduce_sum | solution.py:55
  574.3 7.1 %clamp_convert_fusion = (bf16[256,4096]{1,0:T(8,128)(2,1)}, bf16[256,4096]{1,0:T(8,128)(2,1)}) fusion(bf16[256,4096]{1,0:T(8,128)(2,1)} %param.8, f32[256,4096]{1,0:T(8,128)} %convert_reduce_fusion, bf16[256,4096]{1,0:T(8,128)(2,1)} %param.9), kind=kLoop, calls=%fused_computation.6 | loop fusion | flops 11534336 | bytes 12582912 | tf_op jit(solution)/shard_map/convert_element_type | solution.py:25
  (2 shorter events, 0.0 us)
Async XLA Ops:
  0.6 391.4 %copy-start = (bf16[256,4096]{1,0:T(8,128)(2,1)S(1)}, bf16[256,4096]{1,0:T(8,128)(2,1)}, u32[]{:S(2)}) copy-start(bf16[256,4096]{1,0:T(8,128)(2,1)} %param.7) | copy-start | bytes 6291460
  7.4 384.6 %all-to-all-start = ((bf16[256,8,4096]{2,1,0:T(8,128)(2,1)}), bf16[256,8,4096]{2,1,0:T(8,128)(2,1)}, u32[]{:S(2)}, u32[]{:S(2)}) async-start(bf16[256,8,4096]{2,1,0:T(8,128)(2,1)} %stack.2), calls=%async_computation | async-start | bytes 33554432 | tf_op jit(solution)/shard_map/all_to_all | solution.py:31
  24.1 449.9 %copy-start.1 = (s32[2048]{0:T(1024)S(1)}, s32[2048]{0:T(1024)}, u32[]{:S(2)}) copy-start(s32[2048]{0:T(1024)} %param.10) | copy-start | bytes 24580
  24.1 527.7 %copy-start.2 = (s32[2048]{0:T(1024)S(1)}, s32[2048]{0:T(1024)}, u32[]{:S(2)}) copy-start(s32[2048]{0:T(1024)} %param.11) | copy-start | bytes 24580
